TPU v7x, 768 devices: a whole 4x8x12 slice. The times are simulated.
768 devices in a mesh: group: 24 (over z, core), member: 32 (over y, x).
Axes of the slice: x: 4, y: 8, z: 12, core: 2. Of those that a mesh axis runs over, the one named last changes fastest.
Arguments:
- features: bfloat16 [393216, 512], P(('group', 'member')), may hold values from -6 to 6
- w_self: bfloat16 [512, 512], replicated, may hold values from -0.25 to 0.25
- w_neigh: bfloat16 [512, 512], replicated, may hold values from -0.25 to 0.25
- bias: float32 [512], replicated, may hold values from -3 to 3
- set_members: int32 [196608, 8], P(('group', 'member')), may hold values from 0 to 511
- set_size: int32 [196608], P(('group', 'member')), may hold values from 1 to 8
- cross_list: int32 [24, 32, 24, 16], P('group', 'member'), may hold values from 0 to 255
- inner_list: int32 [24, 32, 32, 16], P('group', 'member'), may hold values from 0 to 383
- ref_slot: int32 [393216, 8], P(('group', 'member')), may hold values from 0 to 511
- ref_count: int32 [393216], P(('group', 'member')), may hold values from 1 to 8
- cotangent: bfloat16 [393216, 512], P(('group', 'member')), may hold values from -6 to 6
Outputs:
- output: bfloat16 [393216, 512], P(('group', 'member'))
- grad_features: bfloat16 [393216, 512], P(('group', 'member'))
- grad_w_self: float32 [512, 512], replicated
- grad_w_neigh: float32 [512, 512], replicated
- grad_bias: float32 [512], replicated
All inputs are finite; a program needn't handle non-finite values.
Results may differ from a plain program's by a relative error of at most 0.0066.
Values may be sent and summed in bfloat16 or wider, within the bound.
A program may use at most 32 MiB of HBM per device.

v0:
```python
import jax
import jax.numpy as jnp
from jax import lax
from jax.sharding import PartitionSpec as P


def one_hot_rows(indices, columns):
    return (indices[:, None] == jnp.arange(columns, dtype=jnp.int32)[None, :]).astype(jnp.bfloat16)


def shards(
    features,
    w_self,
    w_neigh,
    bias,
    set_members,
    set_size,
    cross_list,
    inner_list,
    ref_slot,
    ref_count,
    cotangent,
):
    node_rows, width = features.shape
    set_rows, most = set_members.shape
    group_count = lax.axis_size("group")
    member_count = lax.axis_size("member")
    group_slots = cross_list.shape[3]
    member_slots = inner_list.shape[3]
    ref_width = ref_slot.shape[1]
    slot_total = member_count * member_slots
    relay_total = group_count * group_slots
    node_iota = jnp.arange(node_rows, dtype=jnp.int32)[None, :]
    membership = jnp.zeros((set_rows, node_rows), jnp.float32)
    for position in range(most):
        hit = (set_members[:, position][:, None] == node_iota) & (position < set_size)[:, None]
        membership = membership + hit.astype(jnp.float32)
    membership = membership.astype(jnp.bfloat16)
    agg = jnp.dot(membership, features, preferred_element_type=jnp.float32).astype(jnp.bfloat16)
    cross_rows = cross_list.reshape(-1)
    outgoing = jnp.take(agg, cross_rows, axis=0).reshape(group_count, group_slots, width)
    relay = lax.all_to_all(outgoing, "group", split_axis=0, concat_axis=0, tiled=True).reshape(
        -1, width
    )
    inner_rows = inner_list.reshape(-1)
    passing = jnp.take(relay, inner_rows, axis=0).reshape(member_count, member_slots, width)
    arrived = lax.all_to_all(passing, "member", split_axis=0, concat_axis=0, tiled=True).reshape(
        -1, width
    )
    slot_iota = jnp.arange(slot_total, dtype=jnp.int32)[None, :]
    ref_matrix = jnp.zeros((node_rows, slot_total), jnp.float32)
    for which in range(ref_width):
        hit = (ref_slot[:, which][:, None] == slot_iota) & (which < ref_count)[:, None]
        ref_matrix = ref_matrix + hit.astype(jnp.float32)
    count_f = ref_count.astype(jnp.float32)[:, None]
    total = jnp.dot(ref_matrix.astype(jnp.bfloat16), arrived, preferred_element_type=jnp.float32)
    neigh = (total / count_f).astype(jnp.bfloat16)
    preact = (
        jnp.dot(features, w_self, preferred_element_type=jnp.float32)
        + jnp.dot(neigh, w_neigh, preferred_element_type=jnp.float32)
        + bias
    )
    gate_val = jax.nn.sigmoid(preact)
    output = (preact * gate_val).astype(jnp.bfloat16)
    grad_full = cotangent.astype(jnp.float32) * gate_val * (1.0 + preact * (1.0 - gate_val))
    grad_low = grad_full.astype(jnp.bfloat16)
    grad_neigh = (
        lax.dot_general(
            grad_low, w_neigh, (((1,), (1,)), ((), ())), preferred_element_type=jnp.float32
        )
        / count_f
    )
    grad_slot = lax.dot_general(
        ref_matrix,
        grad_neigh,
        (((0,), (0,)), ((), ())),
        precision=lax.Precision.HIGHEST,
        preferred_element_type=jnp.float32,
    )
    grad_slot = grad_slot.astype(jnp.bfloat16).reshape(member_count, member_slots, width)
    returned = lax.all_to_all(grad_slot, "member", split_axis=0, concat_axis=0, tiled=True).reshape(
        -1, width
    )
    relay_hot = one_hot_rows(inner_rows, relay_total)
    grad_relay = lax.dot_general(
        relay_hot, returned, (((0,), (0,)), ((), ())), preferred_element_type=jnp.float32
    )
    grad_relay = grad_relay.astype(jnp.bfloat16).reshape(group_count, group_slots, width)
    homeward = lax.all_to_all(grad_relay, "group", split_axis=0, concat_axis=0, tiled=True).reshape(
        -1, width
    )
    cross_hot = one_hot_rows(cross_rows, set_rows)
    grad_agg = lax.dot_general(
        cross_hot, homeward, (((0,), (0,)), ((), ())), preferred_element_type=jnp.float32
    ).astype(jnp.bfloat16)
    grad_own = lax.dot_general(
        grad_low, w_self, (((1,), (1,)), ((), ())), preferred_element_type=jnp.float32
    )
    grad_sets = lax.dot_general(
        membership, grad_agg, (((0,), (0,)), ((), ())), preferred_element_type=jnp.float32
    )
    grad_features = (grad_own + grad_sets).astype(jnp.bfloat16)
    grad_ws = lax.dot_general(
        features, grad_low, (((0,), (0,)), ((), ())), preferred_element_type=jnp.float32
    )
    grad_wn = lax.dot_general(
        neigh, grad_low, (((0,), (0,)), ((), ())), preferred_element_type=jnp.float32
    )
    grad_b = jnp.sum(grad_full, axis=0)
    total_ws, total_wn, total_b = lax.psum((grad_ws, grad_wn, grad_b), ("group", "member"))
    return (output, grad_features, total_ws, total_wn, total_b)


def solution(mesh):
    in_specs = (
        P(("group", "member"), None),
        P(),
        P(),
        P(),
        P(("group", "member"), None),
        P(("group", "member")),
        P("group", "member", None, None),
        P("group", "member", None, None),
        P(("group", "member"), None),
        P(("group", "member")),
        P(("group", "member"), None),
    )
    out_specs = (P(("group", "member"), None), P(("group", "member"), None), P(), P(), P())
    return jax.shard_map(shards, mesh=mesh, in_specs=in_specs, out_specs=out_specs, check_vma=False)
```

profile of v0, /device:TPU:1, one launch (start us, length us, event | category | flops | bytes accessed | tf_op | source)
XLA Modules:
  0.0 621.2 jit_solution(17998342007098554822)
XLA Ops:
  7.2 0.8 compare_and_fusion
  8.0 0.1 copy.20
  8.1 0.5 copy-done.11
  8.7 0.1 copy-done.10
  8.7 0.1 reshape.146
  8.9 2.4 convolution_convert_fusion.3
  11.3 2.1 gather_fusion
  13.4 0.9 broadcast_select_fusion.1
  14.2 16.8 %all-to-all-start = ((bf16[24,16,512]{2,1,0:T(8,128)(2,1)}), bf16[24,16,512]{2,1,0:T(8,128)(2,1)S(1)}, u32[]{:S(2)}, u32[]{:S(2)}) async-start(bf16[24,16,512]{2,1,0:T(8,128)(2,1)} %broadcast_select_fusion.1), calls=%async_computation | async-start | bytes 786432 | tf_op jit(solution)/shard_map/all_to_all | solution.py:42
  31.2 0.1 copy.19
  31.4 17.9 %all-to-all-done = bf16[24,16,512]{2,1,0:T(8,128)(2,1)S(1)} async-done(((bf16[24,16,512]{2,1,0:T(8,128)(2,1)}), bf16[24,16,512]{2,1,0:T(8,128)(2,1)S(1)}, u32[]{:S(2)}, u32[]{:S(2)}) %all-to-all-start) | async-done | bytes 393248 | tf_op jit(solution)/shard_map/all_to_all | solution.py:42
  49.3 2.0 gather_fusion.1
  51.3 0.9 broadcast_select_fusion
  52.2 9.8 %all-to-all-start.1 = ((bf16[32,16,512]{2,1,0:T(8,128)(2,1)}), bf16[32,16,512]{2,1,0:T(8,128)(2,1)S(1)}, u32[]{:S(2)}, u32[]{:S(2)}) async-start(bf16[32,16,512]{2,1,0:T(8,128)(2,1)} %broadcast_select_fusion), calls=%async_computation.1 | async-start | bytes 1048576 | tf_op jit(solution)/shard_map/all_to_all | solution.py:47
  62.1 0.4 fusion.28
  62.6 13.4 %all-to-all-done.1 = bf16[32,16,512]{2,1,0:T(8,128)(2,1)S(1)} async-done(((bf16[32,16,512]{2,1,0:T(8,128)(2,1)}), bf16[32,16,512]{2,1,0:T(8,128)(2,1)S(1)}, u32[]{:S(2)}, u32[]{:S(2)}) %all-to-all-start.1) | async-done | bytes 524320 | tf_op jit(solution)/shard_map/all_to_all | solution.py:47
  76.0 2.6 fusion.1
  78.7 1.7 fusion.25
  80.3 0.5 convolution_divide_fusion
  80.8 4.3 convolution_convert_fusion
  85.1 5.9 all-to-all-start.2
  91.1 1.4 fusion.29
  92.5 11.6 %all-to-all-done.2 = bf16[32,16,512]{2,1,0:T(8,128)(2,1)S(1)} async-done(((bf16[32,16,512]{2,1,0:T(8,128)(2,1)}), bf16[32,16,512]{2,1,0:T(8,128)(2,1)S(1)}, u32[]{:S(2)}, u32[]{:S(2)}) %all-to-all-start.2) | async-done | bytes 524320 | tf_op jit(solution)/shard_map/all_to_all | solution.py:81
  104.1 1.2 convolution_convert_fusion.1
  105.3 13.3 %all-to-all-start.3 = ((bf16[24,16,512]{2,1,0:T(8,128)(2,1)}), bf16[24,16,512]{2,1,0:T(8,128)(2,1)S(1)}, u32[]{:S(2)}, u32[]{:S(2)}) async-start(bf16[24,16,512]{2,1,0:T(8,128)(2,1)} %bitcast.25), calls=%async_computation.3 | async-start | bytes 786432 | tf_op jit(solution)/shard_map/all_to_all | solution.py:89
  118.7 1.4 convolution_bitcast_fusion
  120.2 109.1 %psum.23 = f32[512]{0:T(512)} all-reduce(f32[512]{0:T(512)S(1)} %get-tuple-element.17), channel_id=1, replica_groups=mesh['group'=24,'member'=32] {'group','member'}, use_global_device_ids=true, to_apply=%region_3.4 | all-reduce | flops 512 | bytes 4096 | tf_op jit(solution)/shard_map/psum | solution.py:110
  229.4 378.8 %all-reduce.3.cloned.1.call-done = (f32[512,512]{0,1:T(8,128)}, f32[512,512]{1,0:T(8,128)}) async-done(((f32[512,512]{0,1:T(8,128)}, f32[512,512]{1,0:T(8,128)}), (f32[512,512]{0,1:T(8,128)}, f32[512,512]{1,0:T(8,128)})) %all-reduce.3.cloned.1.call-update) | async-done | bytes 2097168 | tf_op jit(solution)/shard_map/psum | solution.py:110
  608.2 2.5 copy.25
  610.8 1.4 fusion.3
  612.2 1.3 fusion.2
  613.4 1.0 copy.28
  (44 shorter events, 0.6 us)
Async XLA Ops:
  7.2 71.5 %copy-start = (bf16[512,512]{1,0:T(8,128)(2,1)S(1)}, bf16[512,512]{1,0:T(8,128)(2,1)}, u32[]{:S(2)}) copy-start(bf16[512,512]{1,0:T(8,128)(2,1)} %param.13) | copy-start | bytes 1572868
  7.2 0.8 copy-start.7
  8.0 0.7 copy-start.11
  8.0 0.7 copy-start.10
  14.2 16.8 %copy-start.6 = (s32[1,1,32,16]{2,3,1,0:T(8,128)S(1)}, s32[1,1,32,16]{2,3,1,0:T(8,128)}, u32[]{:S(2)}) copy-start(s32[1,1,32,16]{2,3,1,0:T(8,128)} %param.18) | copy-start | bytes 6148
  14.2 35.1 %all-to-all-start = ((bf16[24,16,512]{2,1,0:T(8,128)(2,1)}), bf16[24,16,512]{2,1,0:T(8,128)(2,1)S(1)}, u32[]{:S(2)}, u32[]{:S(2)}) async-start(bf16[24,16,512]{2,1,0:T(8,128)(2,1)} %broadcast_select_fusion.1), calls=%async_computation | async-start | bytes 786432 | tf_op jit(solution)/shard_map/all_to_all | solution.py:42
  51.3 10.8 %copy-start.9 = (s32[512]{0:T(512)S(1)}, s32[512]{0:T(512)}, u32[]{:S(2)}) copy-start(s32[512]{0:T(512)} %param.20) | copy-start | bytes 6148
  51.3 10.8 %copy-start.8 = (s32[512,8]{0,1:T(8,128)S(1)}, s32[512,8]{0,1:T(8,128)}, u32[]{:S(2)}) copy-start(s32[512,8]{0,1:T(8,128)} %param.19) | copy-start | bytes 49156
  52.2 9.9 %copy-start.1 = (bf16[512,512]{1,0:T(8,128)(2,1)S(1)}, bf16[512,512]{1,0:T(8,128)(2,1)}, u32[]{:S(2)}) copy-start(bf16[512,512]{1,0:T(8,128)(2,1)} %param.12) | copy-start | bytes 1572868
  52.2 9.9 %copy-start.2 = (bf16[512,512]{1,0:T(8,128)(2,1)S(1)}, bf16[512,512]{1,0:T(8,128)(2,1)}, u32[]{:S(2)}) copy-start(bf16[512,512]{1,0:T(8,128)(2,1)} %param.11) | copy-start | bytes 1572868
  52.2 23.8 %all-to-all-start.1 = ((bf16[32,16,512]{2,1,0:T(8,128)(2,1)}), bf16[32,16,512]{2,1,0:T(8,128)(2,1)S(1)}, u32[]{:S(2)}, u32[]{:S(2)}) async-start(bf16[32,16,512]{2,1,0:T(8,128)(2,1)} %broadcast_select_fusion), calls=%async_computation.1 | async-start | bytes 1048576 | tf_op jit(solution)/shard_map/all_to_all | solution.py:47
  76.0 2.6 copy-start.12
  76.0 2.7 copy-start.13
  78.7 1.7 copy-start.4
  85.1 6.0 copy-start.5
  85.1 19.0 %all-to-all-start.2 = ((bf16[32,16,512]{2,1,0:T(8,128)(2,1)}), bf16[32,16,512]{2,1,0:T(8,128)(2,1)S(1)}, u32[]{:S(2)}, u32[]{:S(2)}) async-start(bf16[32,16,512]{2,1,0:T(8,128)(2,1)} %bitcast.23), calls=%async_computation.2 | async-start | bytes 1048576 | tf_op jit(solution)/shard_map/all_to_all | solution.py:81
  105.3 505.4 %all-to-all-start.3 = ((bf16[24,16,512]{2,1,0:T(8,128)(2,1)}), bf16[24,16,512]{2,1,0:T(8,128)(2,1)S(1)}, u32[]{:S(2)}, u32[]{:S(2)}) async-start(bf16[24,16,512]{2,1,0:T(8,128)(2,1)} %bitcast.25), calls=%async_computation.3 | async-start | bytes 786432 | tf_op jit(solution)/shard_map/all_to_all | solution.py:89
  118.7 489.6 %all-reduce.3.cloned.1.call-start = ((), (), s32[]{:S(2)}) async-start(), calls=%async_computation.4 | async-start | bytes 4194304 | tf_op jit(solution)/shard_map/psum | solution.py:110
  612.2 1.3 copy-start.3
Sparse Core Ops, SparseCore 0:
  125.9 482.2 all-reduce.2
where the time goes:
time: 623 us; the launch traced here: 621 us
  waiting for transfers between devices  422 us (68%)
  blocking collectives  109 us (17%)
  starting transfers between devices  45.9 us (7%)
  matrix products  18.6 us (3%)
  between operations  14.3 us (2%)
  local copies, waits for them, and re-layouts  8.85 us (1%)
    psum x1, waiting for transfers between devices, shards(): lax.psum((grad_ws, grad_wn, grad_b), ('group', 'member'))  379 us
    psum x1, blocking collectives, shards(): lax.psum((grad_ws, grad_wn, grad_b), ('group', 'member'))  109 us
    all_to_all x1, waiting for transfers between devices, shards(): lax.all_to_all(outgoing, 'group', split_axis=0, concat_axis=0, tiled=True)  17.9 us
    all_to_all x1, starting transfers between devices, shards(): lax.all_to_all(outgoing, 'group', split_axis=0, concat_axis=0, tiled=True)  16.8 us
    all_to_all x1, waiting for transfers between devices, shards(): lax.all_to_all(passing, 'member', split_axis=0, concat_axis=0, tiled=True)  13.4 us
    all_to_all x1, starting transfers between devices, shards(): lax.all_to_all(grad_relay, 'group', split_axis=0, concat_axis=0, tiled=True)  13.3 us
  transfers between devices with their start and end apart: 5, of which 4 were waited for; matrix products, arithmetic and copies ran while one was open for 1% of the time, Pallas kernels for 0%

commit v1 on v0

v1 whole, which is shorter than its diff:
```python
import functools

import jax
import jax.numpy as jnp
from jax import lax
from jax.experimental import pallas as pl
from jax.experimental.pallas import tpu as pltpu
from jax.sharding import PartitionSpec as P

MESH = pl.DeviceIdType.MESH
BF = jnp.bfloat16
F32 = jnp.float32
CORES = 2


def dot(a, b, ca=1, cb=0):
    return lax.dot_general(a, b, (((ca,), (cb,)), ((), ())), preferred_element_type=F32)


def kernel(
    groups, members, nx, cap,
    feats, w_self, w_neigh, bias, mem_live, ref_live, cross_row, inner_row, cot,
    out, gfeat, gws, gwn, gbias,
    member_of, ref_of, cross_t, inner_t, send_z, relay, send_m, arrived,
    neigh, low, pre, own, split, back_m, returned, back_z, homeward,
    part, core_send, core_recv, x_send, x_recv, y_send, y_recv, z_recv, whole,
    bias_own, bias_core, bias_x, bias_y, bias_z,
    ssem, rsem,
):
    g = lax.axis_index("group")
    m = lax.axis_index("member")
    z, core = g // CORES, g % CORES
    y, x = m // nx, m % nx
    nz, ny = groups // CORES, members // nx
    nodes, width = feats.shape
    sets = mem_live.shape[0]

    barrier = pltpu.get_barrier_semaphore()

    def greet(axis, count, me):
        def body(k, c):
            peer = lax.rem(me + k, count)
            pl.semaphore_signal(barrier, inc=1, device_id={axis: peer}, device_id_type=MESH)
            return c
        lax.fori_loop(1, count, body, 0)

    greet("group", groups, g)
    greet("member", members, m)

    def remote(src, dst, which, target):
        return pltpu.make_async_remote_copy(
            src_ref=src, dst_ref=dst, send_sem=ssem.at[which], recv_sem=rsem.at[which],
            device_id=target, device_id_type=MESH,
        )

    def landed(ref, which):
        pltpu.make_async_copy(ref, ref, rsem.at[which]).wait()

    def left(ref, which):
        pltpu.make_async_copy(ref, ref, ssem.at[which]).wait()

    def exchange(src, dst, which, axis, count, me):
        def body(k, c):
            peer = lax.rem(me + k, count)
            at = pl.multiple_of(peer * cap, cap)
            to = pl.multiple_of(me * cap, cap)
            remote(src.at[pl.ds(at, cap)], dst.at[pl.ds(to, cap)], which, {axis: peer}).start()
            return c
        lax.fori_loop(1, count, body, 0)
        mine = pl.ds(pl.multiple_of(me * cap, cap), cap)
        dst[mine, :] = src[mine, :]

    lane = lax.broadcasted_iota(jnp.int32, (sets, nodes), 1)
    acc = jnp.zeros((sets, nodes), F32)
    for k in range(mem_live.shape[1]):
        acc += jnp.where(mem_live[:, k:k + 1] == lane, 1.0, 0.0)
    member_of[...] = acc.astype(BF)
    agg = dot(member_of[...], feats[...]).astype(BF)
    relays = groups * cap
    sub = lax.broadcasted_iota(jnp.int32, (sets, relays), 0)
    cross_t[...] = jnp.where(cross_row[...] == sub, 1.0, 0.0).astype(BF)
    send_z[...] = dot(cross_t[...], agg, 0, 0).astype(BF)

    pl.semaphore_wait(barrier, groups + members - 2)
    exchange(send_z, relay, 0, "group", groups, g)

    slots = members * cap
    sub = lax.broadcasted_iota(jnp.int32, (relays, slots), 0)
    inner_t[...] = jnp.where(inner_row[...] == sub, 1.0, 0.0).astype(BF)
    blk = 128
    for b in range(nodes // blk):
        rows = slice(b * blk, (b + 1) * blk)
        lane = lax.broadcasted_iota(jnp.int32, (blk, slots), 1)
        acc = jnp.zeros((blk, slots), F32)
        for k in range(ref_live.shape[1]):
            acc += jnp.where(ref_live[rows, k:k + 1] == lane, 1.0, 0.0)
        ref_of[rows, :] = acc.astype(BF)
    pre[...] = dot(feats[...], w_self[...]) + bias[...]

    landed(relay.at[pl.ds(0, (groups - 1) * cap)], 0)
    send_m[...] = dot(inner_t[...], relay[...], 0, 0).astype(BF)
    exchange(send_m, arrived, 1, "member", members, m)
    landed(arrived.at[pl.ds(0, (members - 1) * cap)], 1)

    total_b = jnp.zeros((1, width), F32)
    for b in range(nodes // blk):
        rows = slice(b * blk, (b + 1) * blk)
        count = jnp.sum(jnp.where(ref_live[rows, :] >= 0, 1.0, 0.0), axis=1, keepdims=True)
        mean = (dot(ref_of[rows, :], arrived[...]) / count).astype(BF)
        neigh[rows, :] = mean
        p = pre[rows, :] + dot(mean, w_neigh[...])
        gate = jax.nn.sigmoid(p)
        out[rows, :] = (p * gate).astype(BF)
        full = cot[rows, :].astype(F32) * gate * (1.0 + p * (1.0 - gate))
        total_b = total_b + jnp.sum(full, axis=0, keepdims=True)
        lowb = full.astype(BF)
        low[rows, :] = lowb
        gn = dot(lowb, w_neigh[...], 1, 1) / count
        hi = gn.astype(BF)
        split[0, rows, :] = hi
        split[1, rows, :] = (gn - hi.astype(F32)).astype(BF)
    back_m[...] = (dot(ref_of[...], split[0], 0, 0) + dot(ref_of[...], split[1], 0, 0)).astype(BF)
    exchange(back_m, returned, 2, "member", members, m)

    part[0] = dot(feats[...], low[...], 0, 0)
    part[1] = dot(neigh[...], low[...], 0, 0)
    sibling = {"group": z * CORES + 1 - core}
    core_send[...] = part[1 - core].astype(BF)
    bias_own[...] = jnp.zeros_like(bias_own)
    for i in range(width // 128):
        bias_own[i:i + 1, :] = total_b[:, i * 128:(i + 1) * 128]
    core_copy = remote(core_send, core_recv, 3, sibling)
    core_copy.start()
    bias_copy = remote(bias_own, bias_core, 4, sibling)
    bias_copy.start()
    own[...] = dot(low[...], w_self[...], 1, 1)
    core_copy.wait()
    bias_copy.wait()

    chunk = width // nx

    def peers(count, me, go):
        def body(k, c):
            go(lax.rem(me + k, count))
            return c
        lax.fori_loop(1, count, body, 0)

    def x_target(p):
        return {"member": y * nx + p}

    def y_target(p):
        return {"member": p * nx + x}

    def z_target(p):
        return {"group": p * CORES + core}

    x_send[...] = (part[core] + core_recv[...].astype(F32)).astype(BF)
    bias_x[x] = bias_own[...] + bias_core[...]

    def go(p):
        at = pl.multiple_of(p * chunk, chunk)
        remote(x_send.at[pl.ds(at, chunk)], x_recv.at[x], 5, x_target(p)).start()
        remote(bias_x.at[x], bias_x.at[x], 6, x_target(p)).start()
    peers(nx, x, go)

    landed(returned.at[pl.ds(0, (members - 1) * cap)], 2)
    back_z[...] = dot(inner_t[...], returned[...]).astype(BF)
    exchange(back_z, homeward, 7, "group", groups, g)

    x_rows = pl.ds(pl.multiple_of(x * chunk, chunk), chunk)
    landed(x_recv.at[pl.ds(0, nx - 1)], 5)
    landed(bias_x.at[pl.ds(0, nx - 1)], 6)
    x_recv[x] = x_send[x_rows, :]
    acc = x_recv[0].astype(F32)
    for i in range(1, nx):
        acc += x_recv[i].astype(F32)
    y_send[...] = acc.astype(BF)
    acc = bias_x[0]
    for i in range(1, nx):
        acc += bias_x[i]
    bias_y[y] = acc

    piece = chunk // ny

    def go(p):
        at = pl.multiple_of(p * piece, piece)
        remote(y_send.at[pl.ds(at, piece)], y_recv.at[y], 8, y_target(p)).start()
        remote(bias_y.at[y], bias_y.at[y], 9, y_target(p)).start()
    peers(ny, y, go)
    landed(y_recv.at[pl.ds(0, ny - 1)], 8)
    landed(bias_y.at[pl.ds(0, ny - 1)], 9)
    y_rows = pl.ds(pl.multiple_of(y * piece, piece), piece)
    y_recv[y] = y_send[y_rows, :]
    acc = y_recv[0].astype(F32)
    for i in range(1, ny):
        acc += y_recv[i].astype(F32)
    z_recv[z] = acc.astype(BF)
    acc = bias_y[0]
    for i in range(1, ny):
        acc += bias_y[i]
    bias_z[z] = acc

    def go(p):
        remote(z_recv.at[z], z_recv.at[z], 10, z_target(p)).start()
        remote(bias_z.at[z], bias_z.at[z], 11, z_target(p)).start()
    peers(nz, z, go)
    landed(z_recv.at[pl.ds(0, nz - 1)], 10)
    landed(bias_z.at[pl.ds(0, nz - 1)], 11)
    acc = z_recv[0].astype(F32)
    for i in range(1, nz):
        acc += z_recv[i].astype(F32)
    piece_rows = pl.ds(pl.multiple_of(x * chunk + y * piece, piece), piece)
    whole[core, piece_rows, :] = acc.astype(BF)
    acc = bias_z[0]
    for i in range(1, nz):
        acc += bias_z[i]
    for i in range(width // 128):
        gbias[:, i * 128:(i + 1) * 128] = acc[i:i + 1, :]

    def go(p):
        ref = whole.at[core, piece_rows]
        remote(ref, ref, 12, y_target(p)).start()
    peers(ny, y, go)

    landed(homeward.at[pl.ds(0, (groups - 1) * cap)], 7)
    grad_agg = dot(cross_t[...], homeward[...]).astype(BF)
    gfeat[...] = (own[...] + dot(member_of[...], grad_agg, 0, 0)).astype(BF)

    landed(whole.at[0, pl.ds(0, (ny - 1) * piece)], 12)

    def go(p):
        ref = whole.at[core, x_rows]
        remote(ref, ref, 13, x_target(p)).start()
    peers(nx, x, go)
    landed(whole.at[0, pl.ds(0, (nx - 1) * chunk)], 13)
    last = remote(whole.at[core], whole.at[core], 14, sibling)
    last.start()
    landed(whole.at[0], 14)
    gws[...] = whole[0].astype(F32)
    gwn[...] = whole[1].astype(F32)

    left(send_z.at[pl.ds(0, (groups - 1) * cap)], 0)
    left(send_m.at[pl.ds(0, (members - 1) * cap)], 1)
    left(back_m.at[pl.ds(0, (members - 1) * cap)], 2)
    left(x_recv.at[pl.ds(0, nx - 1)], 5)
    left(bias_x.at[pl.ds(0, nx - 1)], 6)
    left(back_z.at[pl.ds(0, (groups - 1) * cap)], 7)
    left(y_recv.at[pl.ds(0, ny - 1)], 8)
    left(bias_y.at[pl.ds(0, ny - 1)], 9)
    left(z_recv.at[pl.ds(0, nz - 1)], 10)
    left(bias_z.at[pl.ds(0, nz - 1)], 11)
    left(whole.at[0, pl.ds(0, (ny - 1) * piece)], 12)
    left(whole.at[0, pl.ds(0, (nx - 1) * chunk)], 13)
    left(whole.at[0], 14)


def shards(
    nx, features, w_self, w_neigh, bias, set_members, set_size, cross_list, inner_list,
    ref_slot, ref_count, cotangent,
):
    nodes, width = features.shape
    sets, most = set_members.shape
    groups = lax.axis_size("group")
    members = lax.axis_size("member")
    refs = ref_slot.shape[1]
    cap = cross_list.shape[3]
    ny, nz = members // nx, groups // CORES
    mem_live = jnp.where(jnp.arange(most, dtype=jnp.int32)[None, :] < set_size[:, None], set_members, -1)
    ref_live = jnp.where(jnp.arange(refs, dtype=jnp.int32)[None, :] < ref_count[:, None], ref_slot, -1)
    cross_row = cross_list.reshape(1, groups * cap)
    inner_row = inner_list.reshape(1, members * cap)
    chunk = width // nx
    piece = chunk // ny
    vmem = pl.BlockSpec(memory_space=pltpu.VMEM)
    S = jax.ShapeDtypeStruct
    outs = pl.pallas_call(
        functools.partial(kernel, groups, members, nx, cap),
        out_shape=(
            S((nodes, width), BF), S((nodes, width), BF), S((width, width), F32),
            S((width, width), F32), S((1, width), F32),
        ),
        in_specs=[vmem] * 9,
        out_specs=(vmem,) * 5,
        scratch_shapes=[
            pltpu.VMEM((sets, nodes), BF),
            pltpu.VMEM((nodes, members * cap), BF),
            pltpu.VMEM((sets, groups * cap), BF),
            pltpu.VMEM((groups * cap, members * cap), BF),
            pltpu.VMEM((groups * cap, width), BF),
            pltpu.VMEM((groups * cap, width), BF),
            pltpu.VMEM((members * cap, width), BF),
            pltpu.VMEM((members * cap, width), BF),
            pltpu.VMEM((nodes, width), BF),
            pltpu.VMEM((nodes, width), BF),
            pltpu.VMEM((nodes, width), F32),
            pltpu.VMEM((nodes, width), F32),
            pltpu.VMEM((2, nodes, width), BF),
            pltpu.VMEM((members * cap, width), BF),
            pltpu.VMEM((members * cap, width), BF),
            pltpu.VMEM((groups * cap, width), BF),
            pltpu.VMEM((groups * cap, width), BF),
            pltpu.VMEM((2, width, width), F32),
            pltpu.VMEM((width, width), BF),
            pltpu.VMEM((width, width), BF),
            pltpu.VMEM((width, width), BF),
            pltpu.VMEM((nx, chunk, width), BF),
            pltpu.VMEM((chunk, width), BF),
            pltpu.VMEM((ny, piece, width), BF),
            pltpu.VMEM((nz, piece, width), BF),
            pltpu.VMEM((2, width, width), BF),
            pltpu.VMEM((8, 128), F32),
            pltpu.VMEM((8, 128), F32),
            pltpu.VMEM((nx, 8, 128), F32),
            pltpu.VMEM((ny, 8, 128), F32),
            pltpu.VMEM((nz, 8, 128), F32),
            pltpu.SemaphoreType.DMA((15,)),
            pltpu.SemaphoreType.DMA((15,)),
        ],
        compiler_params=pltpu.CompilerParams(
            collective_id=0, has_side_effects=True, vmem_limit_bytes=48 * 2**20
        ),
    )(features, w_self, w_neigh, bias.reshape(1, width), mem_live, ref_live, cross_row, inner_row, cotangent)
    output, gfeat, gws, gwn, gbias = outs
    return output, gfeat, gws, gwn, gbias.reshape(width)


def solution(mesh):
    nx = 4
    in_specs = (
        P(("group", "member"), None),
        P(),
        P(),
        P(),
        P(("group", "member"), None),
        P(("group", "member")),
        P("group", "member", None, None),
        P("group", "member", None, None),
        P(("group", "member"), None),
        P(("group", "member")),
        P(("group", "member"), None),
    )
    out_specs = (P(("group", "member"), None), P(("group", "member"), None), P(), P(), P())
    return jax.shard_map(
        functools.partial(shards, nx), mesh=mesh, in_specs=in_specs, out_specs=out_specs, check_vma=False
    )
```

time: 623 us -> 120 us (0.19)
  waiting for transfers between devices: 422 us -> 0 us
  Pallas kernels: 0 us -> 109 us
  blocking collectives: 109 us -> 0 us
  starting transfers between devices: 45.9 us -> 0 us
  matrix products: 18.6 us -> 0 us
  between operations: 14.3 us -> 0.71 us
    psum x1 -> x0, waiting for transfers between devices: 379 us -> none  [shards(): lax.psum((grad_ws, grad_wn, grad_b), ('group', 'member'))]
    psum x1 -> x0, blocking collectives: 109 us -> none  [shards(): lax.psum((grad_ws, grad_wn, grad_b), ('group', 'member'))]
    pallas_call x0 -> x1, Pallas kernels: none -> 109 us  [shards(): pl.pallas_call(functools.partial(kernel, groups, members, nx, cap), out_s...]
    all_to_all x4 -> x0, starting transfers between devices: 45.9 us -> none  [the longest x1 16.8 us: shards(): lax.all_to_all(outgoing, 'group', split_axis=0, concat_axis=0, tiled=True)]
    all_to_all x4 -> x0, waiting for transfers between devices: 42.9 us -> none  [the longest x1 17.9 us: shards(): lax.all_to_all(outgoing, 'group', split_axis=0, concat_axis=0, tiled=True)]
    dot_general x11 -> x0, matrix products: 18.6 us -> none  [the longest x1 4.29 us: shards(): lax.dot_general(ref_matrix, grad_neigh, (((0,), (0,)), ((), ())), precisi...]
  transfers between devices with their start and end apart: 5 -> 0, of which waited for: 4 -> 0; matrix products, arithmetic and copies ran while one was open for 1% -> 0% of each run, Pallas kernels for 0% -> 0%
where the time goes in v1:
time: 120 us
  Pallas kernels  109 us (91%)
  local copies, waits for them, and re-layouts  10 us (8%)
    pallas_call x1, Pallas kernels, shards(): pl.pallas_call(functools.partial(kernel, groups, members, nx, cap), out_s...  109 us
    unnamed x29, local copies, waits for them, and re-layouts  9.86 us

profile of v1, /device:TPU:1, one launch (start us, length us, event | category | flops | bytes accessed | tf_op | source)
XLA Modules:
  0.0 120.0 jit_solution(17267843544380456718)
XLA Ops:
  0.6 0.8 copy.22
  1.4 0.0 copy-start.6
  1.4 0.1 reshape.25.cross_row
  1.5 0.6 copy-done.6
  2.1 0.1 copy.23
  2.2 0.0 copy-start.7
  2.2 0.1 reshape.26.inner_row
  2.3 0.6 copy-done.7
  2.9 0.0 copy-start.9
  2.9 0.0 copy-start.5
  2.9 0.0 copy-start.8
  2.9 0.1 copy.20
  3.0 0.5 copy-done.9
  3.6 0.0 copy-start
  3.6 0.0 copy-start.1
  3.6 0.1 fusion.1.mem_live
  3.7 0.0 copy-done.5
  3.7 0.1 copy.21
  3.8 0.0 copy-done.8
  3.8 0.0 copy-start.4
  3.8 0.1 fusion.ref_live
  4.0 0.6 copy-done
  4.6 0.2 copy-done.1
  4.8 0.0 copy-done.4
  4.8 1.0 copy-done.2
  5.8 1.0 copy-done.3
  6.8 109.0 %shard_map.146 = (bf16[512,512]{1,0:T(8,128)(2,1)S(1)}, bf16[512,512]{1,0:T(8,128)(2,1)S(1)}, f32[512,512]{1,0:T(8,128)S(1)}, f32[512,512]{1,0:T(8,128)S(1)}, f32[1,512]{1,0:T(1,128)S(1)}) custom-call(bf16[512,512]{1,0:T(8,128)(2,1)S(1)} %copy-done, bf16[512,512]{1,0:T(8,128)(2,1)S(1)} %copy-done.1, bf16[512,512]{1,0:T(8,128)(2,1)S(1)} %copy-done.2, ...), custom_call_target="tpu_custom_call" | custom-call | tf_op jit(solution)/shard_map/pallas_call | solution.py:276
  115.9 0.8 copy.29
  116.7 0.8 copy.30
  117.4 1.0 copy.31
  118.4 1.0 copy.32
  119.4 0.6 copy.33
  (2 shorter events, 0.0 us)
Async XLA Ops:
  1.4 0.7 copy-start.6
  2.2 0.7 copy-start.7
  2.9 0.7 copy-start.9
  2.9 0.8 copy-start.5
  2.9 0.9 copy-start.8
  3.6 1.0 copy-start
  3.6 1.2 copy-start.1
  3.8 0.9 copy-start.4
  4.8 1.0 copy-start.2
  5.8 1.0 copy-start.3

commit v2 on v0

v2 whole, which is shorter than its diff:
```python
import functools

import jax
import jax.numpy as jnp
from jax import lax
from jax.experimental import pallas as pl
from jax.experimental.pallas import tpu as pltpu
from jax.sharding import PartitionSpec as P

MESH = pl.DeviceIdType.MESH
BF = jnp.bfloat16
F32 = jnp.float32
I32 = jnp.int32
CORES = 2
NCH = 2


def dot(a, b, ca=1, cb=0):
    return lax.dot_general(a, b, (((ca,), (cb,)), ((), ())), preferred_element_type=F32)


def iota(shape, dim):
    return lax.broadcasted_iota(I32, shape, dim)


def flat_row(table):
    cap, n = table.shape
    expand = jnp.where(iota((n, n * cap), 1) // cap == iota((n, n * cap), 0), 1.0, 0.0).astype(BF)
    high = dot((table // 16).astype(F32).astype(BF), expand)
    low = dot((table % 16).astype(F32).astype(BF), expand)
    keep = iota((cap, n * cap), 1) % cap == iota((cap, n * cap), 0)
    return jnp.sum(jnp.where(keep, high * 16.0 + low, 0.0), axis=0, keepdims=True).astype(I32)


def hits(table, count, first, rows):
    entries, n = table.shape
    live = jnp.where(iota((entries, n), 0) < count, table, -1)
    sub = iota((rows, n), 0) + first
    acc = jnp.zeros((rows, n), F32)
    for k in range(entries):
        acc += jnp.where(live[k:k + 1, :] == sub, 1.0, 0.0)
    return acc.astype(BF)


def z_near(nz):
    return 4 if nz % 4 == 0 else nz


def kernel(
    groups, members, nx, cap,
    feats_h, w_self_h, w_neigh_h, bias_h, mem_h, size_h, cross_h, inner_h, ref_h, count_h, cot_h,
    out_h, gfeat_h, grads_h, gbias_h,
    feats, w_self, w_neigh, bias, mem, size, cross, inner, ref, count, cot,
    member_t, member_n, ref_t, ref_n, cross_t, cross_n, inner_t, inner_n, feats_t, inv,
    send_z, relay, send_m, arrived,
    neigh, low, pre, own, split, back_m, returned, back_z, homeward,
    neigh_t, part, core_send, core_recv, x_send, x_recv, y_full, y_send, y_recv, z_recv, z_last, whole,
    out, gfeat, gbias,
    bias_own, bias_core, bias_x, bias_y, bias_z, bias_zl,
    lsem, osem, ssem, rsem, fsem, gsem,
):
    g = lax.axis_index("group")
    m = lax.axis_index("member")
    z, core = g // CORES, g % CORES
    y, x = m // nx, m % nx
    nz, ny = groups // CORES, members // nx
    near = z_near(nz)
    runs = nz // near
    nodes, width = feats.shape
    sets = mem.shape[1]
    wide = width // NCH
    relays, slots = groups * cap, members * cap
    pairs = (
        (mem_h, mem), (size_h, size), (cross_h, cross), (feats_h, feats), (inner_h, inner), (ref_h, ref),
        (count_h, count), (w_self_h, w_self), (bias_h, bias), (w_neigh_h, w_neigh), (cot_h, cot),
    )
    loads = [pltpu.make_async_copy(a, b, lsem.at[i]) for i, (a, b) in enumerate(pairs)]
    for load in loads:
        load.start()

    barrier = pltpu.get_barrier_semaphore()

    def around(count, me, go):
        def body(k, c):
            s = (k + 1) // 2
            go(lax.rem(jnp.where(k % 2 == 1, me + s, me - s + count), count))
            return c
        lax.fori_loop(1, count, body, 0)

    def greet(axis, count, me):
        def go(peer):
            pl.semaphore_signal(barrier, inc=1, device_id={axis: peer}, device_id_type=MESH)
        around(count, me, go)

    greet("group", groups, g)
    greet("member", members, m)

    def remote(src, dst, sems, which, target):
        return pltpu.make_async_remote_copy(
            src_ref=src, dst_ref=dst, send_sem=sems[0].at[which], recv_sem=sems[1].at[which],
            device_id=target, device_id_type=MESH,
        )

    def done(ref, sem):
        pltpu.make_async_copy(ref, ref, sem).wait()

    rows_sems = (fsem, gsem)

    def exchange(src, dst, which, axis, count, me):
        def go(peer):
            at = pl.multiple_of(peer * cap, cap)
            to = pl.multiple_of(me * cap, cap)
            remote(src.at[pl.ds(at, cap)], dst.at[pl.ds(to, cap)], rows_sems, which, {axis: peer}).start()
        around(count, me, go)
        mine = pl.ds(pl.multiple_of(me * cap, cap), cap)
        dst[mine, :] = src[mine, :]

    def others(buf, count):
        return buf.at[0, pl.ds(0, (count - 1) * cap)]

    blk = 64
    loads[0].wait()
    loads[1].wait()
    for b in range(nodes // blk):
        member_t[b * blk:(b + 1) * blk, :] = hits(mem[...], size[...], b * blk, blk)
    member_n[...] = member_t[...].T
    loads[2].wait()
    cross_t[...] = jnp.where(flat_row(cross[...]) == iota((sets, relays), 0), 1.0, 0.0).astype(BF)
    cross_n[...] = cross_t[...].T
    loads[3].wait()
    for h in range(NCH):
        cols = slice(h * wide, (h + 1) * wide)
        agg = dot(member_n[...], feats[:, cols]).astype(BF)
        send_z[h] = dot(cross_n[...], agg).astype(BF)
        if h == 0:
            pl.semaphore_wait(barrier, groups + members - 2)
        exchange(send_z.at[h], relay.at[h], h, "group", groups, g)

    loads[4].wait()
    inner_t[...] = jnp.where(flat_row(inner[...]) == iota((relays, slots), 0), 1.0, 0.0).astype(BF)
    inner_n[...] = inner_t[...].T
    loads[5].wait()
    loads[6].wait()
    blk = 32
    for b in range(slots // blk):
        ref_t[b * blk:(b + 1) * blk, :] = hits(ref[...], count[...], b * blk, blk)
    ref_n[...] = ref_t[...].T
    inv[...] = jnp.broadcast_to(1.0 / count[...].astype(F32), (128, nodes)).T
    feats_t[...] = feats[...].T
    loads[7].wait()
    loads[8].wait()
    pre[...] = dot(feats[...], w_self[...]) + bias[...]
    loads[9].wait()
    loads[10].wait()

    for h in range(NCH):
        done(others(relay, groups), gsem.at[h])
        send_m[h] = dot(inner_n[...], relay[h]).astype(BF)
        exchange(send_m.at[h], arrived.at[h], NCH + h, "member", members, m)

    blk = 128
    total_b = jnp.zeros((1, width), F32)
    for h in range(NCH):
        done(others(arrived, members), gsem.at[NCH + h])
        cols = slice(h * wide, (h + 1) * wide)
        for b in range(nodes // blk):
            rows = slice(b * blk, (b + 1) * blk)
            mean = (dot(ref_n[rows, :], arrived[h]) * inv[rows, 0:1]).astype(BF)
            neigh[rows, cols] = mean
            p = pre[rows, :] + dot(mean, w_neigh[cols, :])
            if h < NCH - 1:
                pre[rows, :] = p
                continue
            gate = jax.nn.sigmoid(p)
            out[rows, :] = (p * gate).astype(BF)
            full = cot[rows, :].astype(F32) * gate * (1.0 + p * (1.0 - gate))
            total_b = total_b + jnp.sum(full, axis=0, keepdims=True)
            low[rows, :] = full.astype(BF)

    sums = (ssem, rsem)
    chunk = width // nx
    piece = chunk // ny
    sibling = {"group": z * CORES + 1 - core}
    x_rows = pl.ds(pl.multiple_of(x * chunk, chunk), chunk)
    y_rows = pl.ds(pl.multiple_of(y * piece, piece), piece)
    piece_rows = pl.ds(pl.multiple_of(x * chunk + y * piece, piece), piece)
    spot, run = z % near, z // near
    bias_sem = 8 * NCH

    def ring(me, count, k):
        return lax.rem(me + k, count)

    def x_target(p):
        return {"member": y * nx + p}

    def y_target(p):
        return {"member": p * nx + x}

    def z_target(p):
        return {"group": p * CORES + core}

    def add_up(buf, n, first=None):
        acc = buf[0].astype(F32) if first is None else first + buf[0].astype(F32)
        for i in range(1, n):
            acc += buf[i].astype(F32)
        return acc

    def core_copy(h):
        return remote(core_send.at[h], core_recv.at[h], sums, h, sibling)

    def bias_copy():
        return remote(bias_own, bias_core, sums, bias_sem, sibling)

    def core_stage(h):
        cols = slice(h * wide, (h + 1) * wide)
        part[0, h] = dot(feats_t[...], low[:, cols])
        part[1, h] = dot(neigh_t[...], low[:, cols])
        core_send[h] = part[1 - core, h].astype(BF)
        core_copy(h).start()
        if h == 0:
            bias_own[...] = jnp.zeros_like(bias_own)
            for i in range(width // 128):
                bias_own[i:i + 1, :] = total_b[:, i * 128:(i + 1) * 128]
            bias_copy().start()

    def x_stage(h):
        core_copy(h).wait()
        total = part[core, h] + core_recv[h].astype(F32)
        part[core, h] = total
        x_send[h] = total.astype(BF)
        for k in range(1, nx):
            p = ring(x, nx, k)
            at = pl.ds(pl.multiple_of(p * chunk, chunk), chunk)
            remote(x_send.at[h, at], x_recv.at[h, k - 1], sums, NCH + h, x_target(p)).start()
        if h == 0:
            bias_copy().wait()
            bias_x[x] = bias_own[...] + bias_core[...]
            for k in range(1, nx):
                p = ring(x, nx, k)
                remote(bias_x.at[x], bias_x.at[x], sums, bias_sem + 1, x_target(p)).start()

    def y_stage(h):
        done(x_recv.at[h], rsem.at[NCH + h])
        total = add_up(x_recv.at[h], nx - 1, part[core, h, x_rows, :])
        y_full[h] = total
        y_send[h] = total.astype(BF)
        for k in range(1, ny):
            p = ring(y, ny, k)
            at = pl.ds(pl.multiple_of(p * piece, piece), piece)
            remote(y_send.at[h, at], y_recv.at[h, k - 1], sums, 2 * NCH + h, y_target(p)).start()
        if h == 0:
            done(bias_x.at[pl.ds(0, nx - 1)], rsem.at[bias_sem + 1])
            bias_y[y] = add_up(bias_x, nx)
            for k in range(1, ny):
                p = ring(y, ny, k)
                remote(bias_y.at[y], bias_y.at[y], sums, bias_sem + 2, y_target(p)).start()

    def z_stage(h):
        done(y_recv.at[h], rsem.at[2 * NCH + h])
        z_recv[h, spot] = add_up(y_recv.at[h], ny - 1, y_full[h, y_rows, :]).astype(BF)
        for k in range(1, near):
            p = run * near + ring(spot, near, k)
            remote(z_recv.at[h, spot], z_recv.at[h, spot], sums, 3 * NCH + h, z_target(p)).start()
        if h == 0:
            done(bias_y.at[pl.ds(0, ny - 1)], rsem.at[bias_sem + 2])
            bias_z[spot] = add_up(bias_y, ny)
            for k in range(1, near):
                p = run * near + ring(spot, near, k)
                remote(bias_z.at[spot], bias_z.at[spot], sums, bias_sem + 3, z_target(p)).start()

    def z_next(h):
        done(z_recv.at[h, pl.ds(0, near - 1)], rsem.at[3 * NCH + h])
        z_last[h, run] = add_up(z_recv.at[h], near).astype(BF)
        for k in range(1, runs):
            p = ring(run, runs, k) * near + spot
            remote(z_last.at[h, run], z_last.at[h, run], sums, 4 * NCH + h, z_target(p)).start()
        if h == 0:
            done(bias_z.at[pl.ds(0, near - 1)], rsem.at[bias_sem + 3])
            bias_zl[run] = add_up(bias_z, near)
            for k in range(1, runs):
                p = ring(run, runs, k) * near + spot
                remote(bias_zl.at[run], bias_zl.at[run], sums, bias_sem + 4, z_target(p)).start()

    def y_back(h):
        done(z_last.at[h, pl.ds(0, runs - 1)], rsem.at[4 * NCH + h])
        whole[core, h, piece_rows, :] = add_up(z_last.at[h], runs).astype(BF)
        at = whole.at[core, h, piece_rows]
        for k in range(1, ny):
            remote(at, at, sums, 5 * NCH + h, y_target(ring(y, ny, k))).start()

    def x_back(h):
        done(whole.at[0, 0, pl.ds(0, (ny - 1) * piece)], rsem.at[5 * NCH + h])
        at = whole.at[core, h, x_rows]
        for k in range(1, nx):
            remote(at, at, sums, 6 * NCH + h, x_target(ring(x, nx, k))).start()

    def core_back(h):
        done(whole.at[0, 0, pl.ds(0, (nx - 1) * chunk)], rsem.at[6 * NCH + h])
        remote(whole.at[core, h], whole.at[core, h], sums, 7 * NCH + h, sibling).start()

    def member_back(h):
        cols = slice(h * wide, (h + 1) * wide)
        for b in range(nodes // blk):
            rows = slice(b * blk, (b + 1) * blk)
            gn = dot(low[rows, :], w_neigh[cols, :], 1, 1) * inv[rows, 0:1]
            hi = gn.astype(BF)
            split[0, rows, :] = hi
            split[1, rows, :] = (gn - hi.astype(F32)).astype(BF)
        back_m[h] = (dot(ref_t[...], split[0]) + dot(ref_t[...], split[1])).astype(BF)

    def member_send(h):
        exchange(back_m.at[h], returned.at[h], 2 * NCH + h, "member", members, m)

    def home(h):
        done(others(returned, members), gsem.at[2 * NCH + h])
        back_z[h] = dot(inner_t[...], returned[h]).astype(BF)
        exchange(back_z.at[h], homeward.at[h], 3 * NCH + h, "group", groups, g)

    def features_back(h):
        cols = slice(h * wide, (h + 1) * wide)
        done(others(homeward, groups), gsem.at[3 * NCH + h])
        grad_agg = dot(cross_t[...], homeward[h]).astype(BF)
        gfeat[:, cols] = (own[:, cols] + dot(member_t[...], grad_agg)).astype(BF)

    stores = [
        pltpu.make_async_copy(out, out_h, osem.at[0]),
        pltpu.make_async_copy(gfeat, gfeat_h, osem.at[1]),
        pltpu.make_async_copy(gbias, gbias_h, osem.at[2]),
        pltpu.make_async_copy(whole.at[core], grads_h.at[core], osem.at[3]),
    ]
    stores[0].start()
    neigh_t[...] = neigh[...].T
    for h in range(NCH):
        core_stage(h)
    for h in range(NCH):
        member_back(h)
        x_stage(h)
    member_send(0)
    own[...] = dot(low[...], w_self[...], 1, 1)
    for h in range(NCH):
        y_stage(h)
    member_send(1)
    home(0)
    for h in range(NCH):
        z_stage(h)
    for h in range(NCH):
        z_next(h)
    home(1)
    for h in range(NCH):
        y_back(h)
    for h in range(NCH):
        x_back(h)
    features_back(0)
    core_back(0)
    features_back(1)
    core_back(1)
    done(bias_zl.at[pl.ds(0, runs - 1)], rsem.at[bias_sem + 4])
    bias_sum = add_up(bias_zl, runs)
    for i in range(width // 128):
        gbias[:, i * 128:(i + 1) * 128] = bias_sum[i:i + 1, :]
    for store in stores[1:]:
        store.start()
    for h in range(NCH):
        done(whole.at[0, 0], rsem.at[7 * NCH + h])
        late = pltpu.make_async_copy(whole.at[1 - core, h], grads_h.at[1 - core, h], osem.at[4 + h])
        late.start()
        stores.append(late)

    for h in range(NCH):
        done(others(send_z, groups), fsem.at[h])
        done(others(send_m, members), fsem.at[NCH + h])
        done(others(back_m, members), fsem.at[2 * NCH + h])
        done(others(back_z, groups), fsem.at[3 * NCH + h])
        done(x_recv.at[h], ssem.at[NCH + h])
        done(y_recv.at[h], ssem.at[2 * NCH + h])
        done(z_recv.at[h, pl.ds(0, near - 1)], ssem.at[3 * NCH + h])
        done(z_last.at[h, pl.ds(0, runs - 1)], ssem.at[4 * NCH + h])
        done(whole.at[0, 0, pl.ds(0, (ny - 1) * piece)], ssem.at[5 * NCH + h])
        done(whole.at[0, 0, pl.ds(0, (nx - 1) * chunk)], ssem.at[6 * NCH + h])
        done(whole.at[0, 0], ssem.at[7 * NCH + h])
    done(bias_x.at[pl.ds(0, nx - 1)], ssem.at[bias_sem + 1])
    done(bias_y.at[pl.ds(0, ny - 1)], ssem.at[bias_sem + 2])
    done(bias_z.at[pl.ds(0, near - 1)], ssem.at[bias_sem + 3])
    done(bias_zl.at[pl.ds(0, runs - 1)], ssem.at[bias_sem + 4])
    for store in stores:
        store.wait()


def finish(out_v, gfeat_v, grads_v, gbias_v, out, gfeat, gws, gwn, gbias, rows, low, full, line, sem):
    wide = grads_v.shape[3]
    parts = [(i, h) for i in range(2) for h in range(NCH)]
    loads = [
        (out_v, rows.at[0]), (gfeat_v, rows.at[1]), (gbias_v, line),
        *((grads_v.at[i, h], low.at[i, h]) for i, h in parts),
    ]
    stores = [(rows.at[0], out), (rows.at[1], gfeat), (line, gbias), (full.at[0], gws), (full.at[1], gwn)]
    loads = [pltpu.make_async_copy(a, b, sem.at[i]) for i, (a, b) in enumerate(loads)]
    stores = [pltpu.make_async_copy(a, b, sem.at[len(loads) + i]) for i, (a, b) in enumerate(stores)]
    for load in loads:
        load.start()
    for i in range(3):
        loads[i].wait()
        stores[i].start()
    for k, (i, h) in enumerate(parts):
        loads[3 + k].wait()
        full[i, :, h * wide:(h + 1) * wide] = low[i, h].astype(F32)
        if h == NCH - 1:
            stores[3 + i].start()
    for store in stores:
        store.wait()


def shards(
    nx, features, w_self, w_neigh, bias, set_members, set_size, cross_list, inner_list,
    ref_slot, ref_count, cotangent,
):
    nodes, width = features.shape
    sets, most = set_members.shape
    groups = lax.axis_size("group")
    members = lax.axis_size("member")
    refs = ref_slot.shape[1]
    cap = cross_list.shape[3]
    ny, nz = members // nx, groups // CORES
    near = z_near(nz)
    chunk = width // nx
    piece = chunk // ny
    wide = width // NCH
    relays, slots = groups * cap, members * cap
    V = pltpu.VMEM
    S = jax.ShapeDtypeStruct
    outs = pl.pallas_call(
        functools.partial(kernel, groups, members, nx, cap),
        out_shape=(
            S((nodes, width), BF), S((nodes, width), BF), S((2, NCH, width, wide), BF), S((1, width), F32),
        ),
        in_specs=[pl.BlockSpec(memory_space=pl.ANY)] * 11,
        out_specs=(pl.BlockSpec(memory_space=pl.ANY),) * 4,
        scratch_shapes=[
            V((nodes, width), BF), V((width, width), BF), V((width, width), BF), V((1, width), F32),
            V((most, sets), I32), V((1, sets), I32), V((cap, groups), I32), V((cap, members), I32),
            V((refs, nodes), I32), V((1, nodes), I32), V((nodes, width), BF),
            V((nodes, sets), BF), V((sets, nodes), BF),
            V((slots, nodes), BF), V((nodes, slots), BF),
            V((sets, relays), BF), V((relays, sets), BF),
            V((relays, slots), BF), V((slots, relays), BF),
            V((width, nodes), BF), V((nodes, 128), F32),
            V((NCH, relays, wide), BF), V((NCH, relays, wide), BF),
            V((NCH, slots, wide), BF), V((NCH, slots, wide), BF),
            V((nodes, width), BF), V((nodes, width), BF),
            V((nodes, width), F32), V((nodes, width), F32),
            V((2, nodes, wide), BF),
            V((NCH, slots, wide), BF), V((NCH, slots, wide), BF),
            V((NCH, relays, wide), BF), V((NCH, relays, wide), BF),
            V((width, nodes), BF), V((2, NCH, width, wide), F32),
            V((NCH, width, wide), BF), V((NCH, width, wide), BF), V((NCH, width, wide), BF),
            V((NCH, nx - 1, chunk, wide), BF), V((NCH, chunk, wide), F32), V((NCH, chunk, wide), BF),
            V((NCH, ny - 1, piece, wide), BF), V((NCH, near, piece, wide), BF), V((NCH, nz // near, piece, wide), BF),
            V((2, NCH, width, wide), BF),
            V((nodes, width), BF), V((nodes, width), BF), V((1, width), F32),
            V((8, 128), F32), V((8, 128), F32), V((nx, 8, 128), F32), V((ny, 8, 128), F32),
            V((near, 8, 128), F32), V((nz // near, 8, 128), F32),
            pltpu.SemaphoreType.DMA((11,)),
            pltpu.SemaphoreType.DMA((4 + NCH,)),
            pltpu.SemaphoreType.DMA((8 * NCH + 5,)),
            pltpu.SemaphoreType.DMA((8 * NCH + 5,)),
            pltpu.SemaphoreType.DMA((4 * NCH,)),
            pltpu.SemaphoreType.DMA((4 * NCH,)),
        ],
        compiler_params=pltpu.CompilerParams(
            collective_id=0, has_side_effects=True, vmem_limit_bytes=60 * 2**20
        ),
    )(
        features, w_self, w_neigh, bias.reshape(1, width), set_members.T, set_size.reshape(1, sets),
        cross_list[0, 0].T, inner_list[0, 0].T, ref_slot.T, ref_count.reshape(1, nodes), cotangent,
    )
    anywhere = pl.BlockSpec(memory_space=pl.ANY)
    output, gfeat, gws, gwn, gbias = pl.pallas_call(
        finish,
        out_shape=(
            S((nodes, width), BF), S((nodes, width), BF), S((width, width), F32), S((width, width), F32),
            S((1, width), F32),
        ),
        in_specs=[anywhere] * 4,
        out_specs=(anywhere,) * 5,
        scratch_shapes=[
            V((2, nodes, width), BF), V((2, NCH, width, wide), BF), V((2, width, width), F32), V((1, width), F32),
            pltpu.SemaphoreType.DMA((8 + 2 * NCH,)),
        ],
        compiler_params=pltpu.CompilerParams(vmem_limit_bytes=60 * 2**20),
    )(*outs)
    return output, gfeat, gws, gwn, gbias.reshape(width)


def solution(mesh):
    nx = 4
    in_specs = (
        P(("group", "member"), None),
        P(),
        P(),
        P(),
        P(("group", "member"), None),
        P(("group", "member")),
        P("group", "member", None, None),
        P("group", "member", None, None),
        P(("group", "member"), None),
        P(("group", "member")),
        P(("group", "member"), None),
    )
    out_specs = (P(("group", "member"), None), P(("group", "member"), None), P(), P(), P())
    return jax.shard_map(
        functools.partial(shards, nx), mesh=mesh, in_specs=in_specs, out_specs=out_specs, check_vma=False
    )
```

time: 623 us -> 96.7 us (0.16)
  waiting for transfers between devices: 422 us -> 0 us
  blocking collectives: 109 us -> 0 us
  Pallas kernels: 0 us -> 95.9 us
  starting transfers between devices: 45.9 us -> 0 us
  matrix products: 18.6 us -> 0 us
  between operations: 14.3 us -> 0.64 us
  local copies, waits for them, and re-layouts: 8.85 us -> 0 us
    psum x1 -> x0, waiting for transfers between devices: 379 us -> none  [shards(): lax.psum((grad_ws, grad_wn, grad_b), ('group', 'member'))]
    psum x1 -> x0, blocking collectives: 109 us -> none  [shards(): lax.psum((grad_ws, grad_wn, grad_b), ('group', 'member'))]
    pallas_call x0 -> x2, Pallas kernels: none -> 95.9 us  [the longest x1 93.1 us: shards(): pl.pallas_call(functools.partial(kernel, groups, members, nx, cap), out_s...]
    all_to_all x4 -> x0, starting transfers between devices: 45.9 us -> none  [the longest x1 16.8 us: shards(): lax.all_to_all(outgoing, 'group', split_axis=0, concat_axis=0, tiled=True)]
    all_to_all x4 -> x0, waiting for transfers between devices: 42.9 us -> none  [the longest x1 17.9 us: shards(): lax.all_to_all(outgoing, 'group', split_axis=0, concat_axis=0, tiled=True)]
    dot_general x11 -> x0, matrix products: 18.6 us -> none  [the longest x1 4.29 us: shards(): lax.dot_general(ref_matrix, grad_neigh, (((0,), (0,)), ((), ())), precisi...]
  transfers between devices with their start and end apart: 5 -> 0, of which waited for: 4 -> 0; matrix products, arithmetic and copies ran while one was open for 1% -> 0% of each run, Pallas kernels for 0% -> 0%
where the time goes in v2:
time: 96.7 us; the launch traced here: 96.6 us
  Pallas kernels  95.9 us (99%)
    pallas_call x1, Pallas kernels, shards(): pl.pallas_call(functools.partial(kernel, groups, members, nx, cap), out_s...  93.1 us
    pallas_call x1, Pallas kernels, shards(): pl.pallas_call(finish, out_shape=(S((nodes, width), BF), S((nodes, width)...  2.81 us

profile of v2, /device:TPU:1, one launch (start us, length us, event | category | flops | bytes accessed | tf_op | source)
XLA Modules:
  0.0 96.6 jit_solution(8378306775292002726)
XLA Ops:
  0.6 93.1 %shard_map.146 = (bf16[512,512]{1,0:T(8,128)(2,1)}, bf16[512,512]{1,0:T(8,128)(2,1)}, bf16[2,2,512,256]{3,2,1,0:T(8,128)(2,1)}, f32[1,512]{1,0:T(1,128)}) custom-call(bf16[512,512]{1,0:T(8,128)(2,1)} %feats_h.1, bf16[512,512]{1,0:T(8,128)(2,1)} %w_self_h.1, bf16[512,512]{1,0:T(8,128)(2,1)} %w_neigh_h.1, f32[1,512]{1,0:T(1,128)} %bitcast.16, ...), custom_call_target="tpu_custom_call" | custom-call | tf_op jit(solution)/shard_map/pallas_call | solution.py:431
  93.8 2.8 %shard_map.147 = (bf16[512,512]{1,0:T(8,128)(2,1)}, bf16[512,512]{1,0:T(8,128)(2,1)}, f32[512,512]{1,0:T(8,128)}, f32[512,512]{1,0:T(8,128)}, f32[1,512]{1,0:T(1,128)}) custom-call(bf16[512,512]{1,0:T(8,128)(2,1)} %get-tuple-element.14.out_v, bf16[512,512]{1,0:T(8,128)(2,1)} %get-tuple-element.15.gfeat_v, ...), custom_call_target="tpu_custom_call" | custom-call | tf_op jit(solution)/shard_map/pallas_call | solution.py:477

commit v3 on v2

v3 whole, which is shorter than its diff:
```python
import functools

import jax
import jax.numpy as jnp
from jax import lax
from jax.experimental import pallas as pl
from jax.experimental.pallas import tpu as pltpu
from jax.sharding import PartitionSpec as P

MESH = pl.DeviceIdType.MESH
BF = jnp.bfloat16
F32 = jnp.float32
I32 = jnp.int32
CORES = 2
FCH = 4
BCH = 4
ACH = 2


def dot(a, b, ca=1, cb=0):
    return lax.dot_general(a, b, (((ca,), (cb,)), ((), ())), preferred_element_type=F32)


def iota(shape, dim):
    return lax.broadcasted_iota(I32, shape, dim)


def flat_row(table):
    cap, n = table.shape
    expand = jnp.where(iota((n, n * cap), 1) // cap == iota((n, n * cap), 0), 1.0, 0.0).astype(BF)
    high = dot((table // 16).astype(F32).astype(BF), expand)
    low = dot((table % 16).astype(F32).astype(BF), expand)
    keep = iota((cap, n * cap), 1) % cap == iota((cap, n * cap), 0)
    return jnp.sum(jnp.where(keep, high * 16.0 + low, 0.0), axis=0, keepdims=True).astype(I32)


def hits(table, count, first, rows):
    entries, n = table.shape
    live = jnp.where(iota((entries, n), 0) < count, table, -1)
    sub = iota((rows, n), 0) + first
    acc = jnp.zeros((rows, n), F32)
    for k in range(entries):
        acc += jnp.where(live[k:k + 1, :] == sub, 1.0, 0.0)
    return acc.astype(BF)


def z_near(nz):
    return 4 if nz % 4 == 0 else nz


def kernel(
    groups, members, nx, cap,
    feats_h, w_self_h, w_neigh_h, bias_h, mem_h, size_h, cross_h, inner_h, ref_h, count_h, cot_h,
    out_h, gfeat_h, grads_h, gbias_h,
    feats, w_self, w_neigh, bias, mem, size, cross, inner, ref, count, cot,
    member_t, member_n, ref_t, ref_n, cross_t, cross_n, inner_t, inner_n, left, inv,
    send_z, relay, send_m, arrived,
    neigh, low, pre, own, split, back_m, returned, back_z, homeward,
    part, core_send, core_recv, x_send, x_recv, y_full, y_send, y_recv, z_recv, z_last, whole,
    out, gfeat, gbias,
    bias_own, bias_core, bias_x, bias_y, bias_z, bias_zl,
    lsem, osem, ssem, rsem, fsem, gsem,
):
    g = lax.axis_index("group")
    m = lax.axis_index("member")
    z, core = g // CORES, g % CORES
    y, x = m // nx, m % nx
    nz, ny = groups // CORES, members // nx
    near = z_near(nz)
    runs = nz // near
    nodes, width = feats.shape
    sets = mem.shape[1]
    fwide, bwide, awide = width // FCH, width // BCH, width // ACH
    relays, slots = groups * cap, members * cap
    pairs = (
        (mem_h, mem), (size_h, size), (cross_h, cross), (feats_h, feats), (inner_h, inner), (ref_h, ref),
        (count_h, count), (w_self_h, w_self), (bias_h, bias), (w_neigh_h, w_neigh), (cot_h, cot),
    )
    loads = [pltpu.make_async_copy(a, b, lsem.at[i]) for i, (a, b) in enumerate(pairs)]
    for load in loads:
        load.start()

    barrier = pltpu.get_barrier_semaphore()

    def around(count, me, go):
        def body(k, c):
            s = (k + 1) // 2
            go(lax.rem(jnp.where(k % 2 == 1, me + s, me - s + count), count))
            return c
        lax.fori_loop(1, count, body, 0)

    def greet(axis, count, me):
        def go(peer):
            pl.semaphore_signal(barrier, inc=1, device_id={axis: peer}, device_id_type=MESH)
        around(count, me, go)

    greet("group", groups, g)
    greet("member", members, m)

    def remote(src, dst, sems, which, target):
        return pltpu.make_async_remote_copy(
            src_ref=src, dst_ref=dst, send_sem=sems[0].at[which], recv_sem=sems[1].at[which],
            device_id=target, device_id_type=MESH,
        )

    def done(ref, sem):
        pltpu.make_async_copy(ref, ref, sem).wait()

    rows_sems = (fsem, gsem)

    def exchange(src, dst, which, axis, count, me):
        def go(peer):
            at = pl.multiple_of(peer * cap, cap)
            to = pl.multiple_of(me * cap, cap)
            remote(src.at[pl.ds(at, cap)], dst.at[pl.ds(to, cap)], rows_sems, which, {axis: peer}).start()
        around(count, me, go)
        mine = pl.ds(pl.multiple_of(me * cap, cap), cap)
        dst[mine, :] = src[mine, :]

    def others(buf, count):
        return buf.at[0, pl.ds(0, (count - 1) * cap)]

    blk = 64
    loads[0].wait()
    loads[1].wait()
    for b in range(nodes // blk):
        member_t[b * blk:(b + 1) * blk, :] = hits(mem[...], size[...], b * blk, blk)
    member_n[...] = member_t[...].T
    loads[2].wait()
    cross_t[...] = jnp.where(flat_row(cross[...]) == iota((sets, relays), 0), 1.0, 0.0).astype(BF)
    cross_n[...] = cross_t[...].T
    loads[3].wait()
    for h in range(FCH):
        cols = slice(h * fwide, (h + 1) * fwide)
        agg = dot(member_n[...], feats[:, cols]).astype(BF)
        send_z[h] = dot(cross_n[...], agg).astype(BF)
        if h == 0:
            pl.semaphore_wait(barrier, groups + members - 2)
        exchange(send_z.at[h], relay.at[h], h, "group", groups, g)

    loads[4].wait()
    inner_t[...] = jnp.where(flat_row(inner[...]) == iota((relays, slots), 0), 1.0, 0.0).astype(BF)
    inner_n[...] = inner_t[...].T
    loads[5].wait()
    loads[6].wait()
    blk = 32
    for b in range(slots // blk):
        ref_t[b * blk:(b + 1) * blk, :] = hits(ref[...], count[...], b * blk, blk)
    ref_n[...] = ref_t[...].T
    inv[...] = jnp.broadcast_to(1.0 / count[...].astype(F32), (128, nodes)).T
    left[0] = feats[...].T
    loads[7].wait()
    loads[8].wait()
    pre[...] = dot(feats[...], w_self[...]) + bias[...]
    loads[9].wait()
    loads[10].wait()

    for h in range(FCH):
        done(others(relay, groups), gsem.at[h])
        send_m[h] = dot(inner_n[...], relay[h]).astype(BF)
        exchange(send_m.at[h], arrived.at[h], FCH + h, "member", members, m)

    blk = 128
    for h in range(FCH):
        done(others(arrived, members), gsem.at[FCH + h])
        cols = slice(h * fwide, (h + 1) * fwide)
        for b in range(nodes // blk):
            rows = slice(b * blk, (b + 1) * blk)
            mean = (dot(ref_n[rows, :], arrived[h]) * inv[rows, 0:1]).astype(BF)
            neigh[rows, cols] = mean
            if h < FCH - 1:
                pre[rows, :] += dot(mean, w_neigh[cols, :])
        left[1, cols, :] = neigh[:, cols].T

    sums = (ssem, rsem)
    chunk = width // nx
    piece = chunk // ny
    sibling = {"group": z * CORES + 1 - core}
    x_rows = pl.ds(pl.multiple_of(x * chunk, chunk), chunk)
    y_rows = pl.ds(pl.multiple_of(y * piece, piece), piece)
    piece_rows = pl.ds(pl.multiple_of(x * chunk + y * piece, piece), piece)
    spot, run = z % near, z // near
    bias_sem = 8 * ACH
    bias_own[...] = jnp.zeros_like(bias_own)

    def ring(me, count, k):
        return lax.rem(me + k, count)

    def x_target(p):
        return {"member": y * nx + p}

    def y_target(p):
        return {"member": p * nx + x}

    def z_target(p):
        return {"group": p * CORES + core}

    def add_up(buf, n, first=None):
        acc = buf[0].astype(F32) if first is None else first + buf[0].astype(F32)
        for i in range(1, n):
            acc += buf[i].astype(F32)
        return acc

    def core_copy(h):
        return remote(core_send.at[h], core_recv.at[h], sums, h, sibling)

    def bias_copy():
        return remote(bias_own, bias_core, sums, bias_sem, sibling)

    def layer(h):
        cols = slice(h * awide, (h + 1) * awide)
        late = slice((FCH - 1) * fwide, width)
        total = jnp.zeros((1, awide), F32)
        for b in range(nodes // blk):
            rows = slice(b * blk, (b + 1) * blk)
            p = pre[rows, cols] + dot(neigh[rows, late], w_neigh[late, cols])
            gate = jax.nn.sigmoid(p)
            out[rows, cols] = (p * gate).astype(BF)
            full = cot[rows, cols].astype(F32) * gate * (1.0 + p * (1.0 - gate))
            total = total + jnp.sum(full, axis=0, keepdims=True)
            low[rows, cols] = full.astype(BF)
        for i in range(awide // 128):
            at = h * (awide // 128) + i
            bias_own[at:at + 1, :] = total[:, i * 128:(i + 1) * 128]

    def core_stage(h):
        cols = slice(h * awide, (h + 1) * awide)
        layer(h)
        core_send[h] = dot(left[1 - core], low[:, cols]).astype(BF)
        core_copy(h).start()
        part[h] = dot(left[core], low[:, cols])
        if h == ACH - 1:
            bias_copy().start()

    def x_stage(h):
        core_copy(h).wait()
        total = part[h] + core_recv[h].astype(F32)
        part[h] = total
        x_send[h] = total.astype(BF)
        for k in range(1, nx):
            p = ring(x, nx, k)
            at = pl.ds(pl.multiple_of(p * chunk, chunk), chunk)
            remote(x_send.at[h, at], x_recv.at[h, k - 1], sums, ACH + h, x_target(p)).start()
        if h == ACH - 1:
            bias_copy().wait()
            bias_x[x] = bias_own[...] + bias_core[...]
            for k in range(1, nx):
                p = ring(x, nx, k)
                remote(bias_x.at[x], bias_x.at[x], sums, bias_sem + 1, x_target(p)).start()

    def y_stage(h):
        done(x_recv.at[h], rsem.at[ACH + h])
        total = add_up(x_recv.at[h], nx - 1, part[h, x_rows, :])
        y_full[h] = total
        y_send[h] = total.astype(BF)
        for k in range(1, ny):
            p = ring(y, ny, k)
            at = pl.ds(pl.multiple_of(p * piece, piece), piece)
            remote(y_send.at[h, at], y_recv.at[h, k - 1], sums, 2 * ACH + h, y_target(p)).start()
        if h == ACH - 1:
            done(bias_x.at[pl.ds(0, nx - 1)], rsem.at[bias_sem + 1])
            bias_y[y] = add_up(bias_x, nx)
            for k in range(1, ny):
                p = ring(y, ny, k)
                remote(bias_y.at[y], bias_y.at[y], sums, bias_sem + 2, y_target(p)).start()

    def z_stage(h):
        done(y_recv.at[h], rsem.at[2 * ACH + h])
        z_recv[h, spot] = add_up(y_recv.at[h], ny - 1, y_full[h, y_rows, :]).astype(BF)
        for k in range(1, near):
            p = run * near + ring(spot, near, k)
            remote(z_recv.at[h, spot], z_recv.at[h, spot], sums, 3 * ACH + h, z_target(p)).start()
        if h == ACH - 1:
            done(bias_y.at[pl.ds(0, ny - 1)], rsem.at[bias_sem + 2])
            bias_z[spot] = add_up(bias_y, ny)
            for k in range(1, near):
                p = run * near + ring(spot, near, k)
                remote(bias_z.at[spot], bias_z.at[spot], sums, bias_sem + 3, z_target(p)).start()

    def z_next(h):
        done(z_recv.at[h, pl.ds(0, near - 1)], rsem.at[3 * ACH + h])
        z_last[h, run] = add_up(z_recv.at[h], near).astype(BF)
        for k in range(1, runs):
            p = ring(run, runs, k) * near + spot
            remote(z_last.at[h, run], z_last.at[h, run], sums, 4 * ACH + h, z_target(p)).start()
        if h == ACH - 1:
            done(bias_z.at[pl.ds(0, near - 1)], rsem.at[bias_sem + 3])
            bias_zl[run] = add_up(bias_z, near)
            for k in range(1, runs):
                p = ring(run, runs, k) * near + spot
                remote(bias_zl.at[run], bias_zl.at[run], sums, bias_sem + 4, z_target(p)).start()

    def y_back(h):
        done(z_last.at[h, pl.ds(0, runs - 1)], rsem.at[4 * ACH + h])
        whole[core, h, piece_rows, :] = add_up(z_last.at[h], runs).astype(BF)
        at = whole.at[core, h, piece_rows]
        for k in range(1, ny):
            remote(at, at, sums, 5 * ACH + h, y_target(ring(y, ny, k))).start()

    def x_back(h):
        done(whole.at[0, 0, pl.ds(0, (ny - 1) * piece)], rsem.at[5 * ACH + h])
        at = whole.at[core, h, x_rows]
        for k in range(1, nx):
            remote(at, at, sums, 6 * ACH + h, x_target(ring(x, nx, k))).start()

    def core_back(h):
        done(whole.at[0, 0, pl.ds(0, (nx - 1) * chunk)], rsem.at[6 * ACH + h])
        remote(whole.at[core, h], whole.at[core, h], sums, 7 * ACH + h, sibling).start()

    def member_back(h):
        cols = slice(h * bwide, (h + 1) * bwide)
        for b in range(nodes // blk):
            rows = slice(b * blk, (b + 1) * blk)
            gn = dot(low[rows, :], w_neigh[cols, :], 1, 1) * inv[rows, 0:1]
            hi = gn.astype(BF)
            split[0, rows, :] = hi
            split[1, rows, :] = (gn - hi.astype(F32)).astype(BF)
        back_m[h] = (dot(ref_t[...], split[0]) + dot(ref_t[...], split[1])).astype(BF)

    def member_send(h):
        exchange(back_m.at[h], returned.at[h], 2 * FCH + h, "member", members, m)

    def home(h):
        done(others(returned, members), gsem.at[2 * FCH + h])
        back_z[h] = dot(inner_t[...], returned[h]).astype(BF)
        exchange(back_z.at[h], homeward.at[h], 2 * FCH + BCH + h, "group", groups, g)

    def features_back(h):
        cols = slice(h * bwide, (h + 1) * bwide)
        done(others(homeward, groups), gsem.at[2 * FCH + BCH + h])
        grad_agg = dot(cross_t[...], homeward[h]).astype(BF)
        gfeat[:, cols] = (own[:, cols] + dot(member_t[...], grad_agg)).astype(BF)

    stores = [
        pltpu.make_async_copy(out, out_h, osem.at[0]),
        pltpu.make_async_copy(gfeat, gfeat_h, osem.at[1]),
        pltpu.make_async_copy(gbias, gbias_h, osem.at[2]),
        pltpu.make_async_copy(whole.at[core], grads_h.at[core], osem.at[3]),
    ]
    core_stage(0)
    core_stage(1)
    stores[0].start()
    member_back(0)
    member_back(1)
    x_stage(0)
    member_back(2)
    member_back(3)
    x_stage(1)
    own[...] = dot(low[...], w_self[...], 1, 1)
    y_stage(0)
    y_stage(1)
    member_send(0)
    member_send(1)
    member_send(2)
    member_send(3)
    z_stage(0)
    z_stage(1)
    z_next(0)
    z_next(1)
    home(0)
    home(1)
    y_back(0)
    home(2)
    y_back(1)
    home(3)
    x_back(0)
    x_back(1)
    features_back(0)
    features_back(1)
    features_back(2)
    core_back(0)
    features_back(3)
    core_back(1)
    done(bias_zl.at[pl.ds(0, runs - 1)], rsem.at[bias_sem + 4])
    bias_sum = add_up(bias_zl, runs)
    for i in range(width // 128):
        gbias[:, i * 128:(i + 1) * 128] = bias_sum[i:i + 1, :]
    for store in stores[1:]:
        store.start()
    for h in range(ACH):
        done(whole.at[0, 0], rsem.at[7 * ACH + h])
        late = pltpu.make_async_copy(whole.at[1 - core, h], grads_h.at[1 - core, h], osem.at[4 + h])
        late.start()
        stores.append(late)

    for h in range(FCH):
        done(others(send_z, groups), fsem.at[h])
        done(others(send_m, members), fsem.at[FCH + h])
    for h in range(BCH):
        done(others(back_m, members), fsem.at[2 * FCH + h])
        done(others(back_z, groups), fsem.at[2 * FCH + BCH + h])
    for h in range(ACH):
        done(x_recv.at[h], ssem.at[ACH + h])
        done(y_recv.at[h], ssem.at[2 * ACH + h])
        done(z_recv.at[h, pl.ds(0, near - 1)], ssem.at[3 * ACH + h])
        done(z_last.at[h, pl.ds(0, runs - 1)], ssem.at[4 * ACH + h])
        done(whole.at[0, 0, pl.ds(0, (ny - 1) * piece)], ssem.at[5 * ACH + h])
        done(whole.at[0, 0, pl.ds(0, (nx - 1) * chunk)], ssem.at[6 * ACH + h])
        done(whole.at[0, 0], ssem.at[7 * ACH + h])
    done(bias_x.at[pl.ds(0, nx - 1)], ssem.at[bias_sem + 1])
    done(bias_y.at[pl.ds(0, ny - 1)], ssem.at[bias_sem + 2])
    done(bias_z.at[pl.ds(0, near - 1)], ssem.at[bias_sem + 3])
    done(bias_zl.at[pl.ds(0, runs - 1)], ssem.at[bias_sem + 4])
    for store in stores:
        store.wait()


def finish(out_v, gfeat_v, grads_v, gbias_v, out, gfeat, gws, gwn, gbias, rows, low, full, line, sem):
    wide = grads_v.shape[3]
    parts = [(i, h) for i in range(2) for h in range(ACH)]
    loads = [
        *((grads_v.at[i, h], low.at[i, h]) for i, h in parts),
        (out_v, rows.at[0]), (gfeat_v, rows.at[1]), (gbias_v, line),
    ]
    stores = [
        *((full.at[i, h], (gws, gwn)[i].at[:, pl.ds(h * wide, wide)]) for i, h in parts),
        (rows.at[0], out), (rows.at[1], gfeat), (line, gbias),
    ]
    loads = [pltpu.make_async_copy(a, b, sem.at[i]) for i, (a, b) in enumerate(loads)]
    stores = [pltpu.make_async_copy(a, b, sem.at[len(loads) + i]) for i, (a, b) in enumerate(stores)]
    for load in loads:
        load.start()
    for k, (load, store) in enumerate(zip(loads, stores)):
        load.wait()
        if k < len(parts):
            i, h = parts[k]
            full[i, h] = low[i, h].astype(F32)
        store.start()
    for store in stores:
        store.wait()


def shards(
    nx, features, w_self, w_neigh, bias, set_members, set_size, cross_list, inner_list,
    ref_slot, ref_count, cotangent,
):
    nodes, width = features.shape
    sets, most = set_members.shape
    groups = lax.axis_size("group")
    members = lax.axis_size("member")
    refs = ref_slot.shape[1]
    cap = cross_list.shape[3]
    ny, nz = members // nx, groups // CORES
    near = z_near(nz)
    chunk = width // nx
    piece = chunk // ny
    fwide, bwide, awide = width // FCH, width // BCH, width // ACH
    relays, slots = groups * cap, members * cap
    V = pltpu.VMEM
    S = jax.ShapeDtypeStruct
    outs = pl.pallas_call(
        functools.partial(kernel, groups, members, nx, cap),
        out_shape=(
            S((nodes, width), BF), S((nodes, width), BF), S((2, ACH, width, awide), BF), S((1, width), F32),
        ),
        in_specs=[pl.BlockSpec(memory_space=pl.ANY)] * 11,
        out_specs=(pl.BlockSpec(memory_space=pl.ANY),) * 4,
        scratch_shapes=[
            V((nodes, width), BF), V((width, width), BF), V((width, width), BF), V((1, width), F32),
            V((most, sets), I32), V((1, sets), I32), V((cap, groups), I32), V((cap, members), I32),
            V((refs, nodes), I32), V((1, nodes), I32), V((nodes, width), BF),
            V((nodes, sets), BF), V((sets, nodes), BF),
            V((slots, nodes), BF), V((nodes, slots), BF),
            V((sets, relays), BF), V((relays, sets), BF),
            V((relays, slots), BF), V((slots, relays), BF),
            V((2, width, nodes), BF), V((nodes, 128), F32),
            V((FCH, relays, fwide), BF), V((FCH, relays, fwide), BF),
            V((FCH, slots, fwide), BF), V((FCH, slots, fwide), BF),
            V((nodes, width), BF), V((nodes, width), BF),
            V((nodes, width), F32), V((nodes, width), F32),
            V((2, nodes, bwide), BF),
            V((BCH, slots, bwide), BF), V((BCH, slots, bwide), BF),
            V((BCH, relays, bwide), BF), V((BCH, relays, bwide), BF),
            V((ACH, width, awide), F32),
            V((ACH, width, awide), BF), V((ACH, width, awide), BF), V((ACH, width, awide), BF),
            V((ACH, nx - 1, chunk, awide), BF), V((ACH, chunk, awide), F32), V((ACH, chunk, awide), BF),
            V((ACH, ny - 1, piece, awide), BF), V((ACH, near, piece, awide), BF), V((ACH, nz // near, piece, awide), BF),
            V((2, ACH, width, awide), BF),
            V((nodes, width), BF), V((nodes, width), BF), V((1, width), F32),
            V((8, 128), F32), V((8, 128), F32), V((nx, 8, 128), F32), V((ny, 8, 128), F32),
            V((near, 8, 128), F32), V((nz // near, 8, 128), F32),
            pltpu.SemaphoreType.DMA((11,)),
            pltpu.SemaphoreType.DMA((4 + ACH,)),
            pltpu.SemaphoreType.DMA((8 * ACH + 5,)),
            pltpu.SemaphoreType.DMA((8 * ACH + 5,)),
            pltpu.SemaphoreType.DMA((2 * FCH + 2 * BCH,)),
            pltpu.SemaphoreType.DMA((2 * FCH + 2 * BCH,)),
        ],
        compiler_params=pltpu.CompilerParams(
            collective_id=0, has_side_effects=True, vmem_limit_bytes=60 * 2**20
        ),
    )(
        features, w_self, w_neigh, bias.reshape(1, width), set_members.T, set_size.reshape(1, sets),
        cross_list[0, 0].T, inner_list[0, 0].T, ref_slot.T, ref_count.reshape(1, nodes), cotangent,
    )
    anywhere = pl.BlockSpec(memory_space=pl.ANY)
    output, gfeat, gws, gwn, gbias = pl.pallas_call(
        finish,
        out_shape=(
            S((nodes, width), BF), S((nodes, width), BF), S((width, width), F32), S((width, width), F32),
            S((1, width), F32),
        ),
        in_specs=[anywhere] * 4,
        out_specs=(anywhere,) * 5,
        scratch_shapes=[
            V((2, nodes, width), BF), V((2, ACH, width, awide), BF), V((2, ACH, width, awide), F32), V((1, width), F32),
            pltpu.SemaphoreType.DMA((6 + 4 * ACH,)),
        ],
        compiler_params=pltpu.CompilerParams(vmem_limit_bytes=60 * 2**20),
    )(*outs)
    return output, gfeat, gws, gwn, gbias.reshape(width)


def solution(mesh):
    nx = 4
    in_specs = (
        P(("group", "member"), None),
        P(),
        P(),
        P(),
        P(("group", "member"), None),
        P(("group", "member")),
        P("group", "member", None, None),
        P("group", "member", None, None),
        P(("group", "member"), None),
        P(("group", "member")),
        P(("group", "member"), None),
    )
    out_specs = (P(("group", "member"), None), P(("group", "member"), None), P(), P(), P())
    return jax.shard_map(
        functools.partial(shards, nx), mesh=mesh, in_specs=in_specs, out_specs=out_specs, check_vma=False
    )
```

time: 96.7 us -> 91.4 us (0.945)
  Pallas kernels: 95.9 us -> 90.6 us
    pallas_call x1, Pallas kernels: 93.1 us -> 87.8 us  [shards(): pl.pallas_call(functools.partial(kernel, groups, members, nx, cap), out_s...]
where the time goes in v3:
time: 91.4 us; the launch traced here: 91.3 us
  Pallas kernels  90.6 us (99%)
    pallas_call x1, Pallas kernels, shards(): pl.pallas_call(functools.partial(kernel, groups, members, nx, cap), out_s...  87.8 us
    pallas_call x1, Pallas kernels, shards(): pl.pallas_call(finish, out_shape=(S((nodes, width), BF), S((nodes, width)...  2.77 us

profile of v3, /device:TPU:1, one launch (start us, length us, event | category | flops | bytes accessed | tf_op | source)
XLA Modules:
  0.0 91.3 jit_solution(2873186830380939627)
XLA Ops:
  0.6 87.8 %shard_map.146 = (bf16[512,512]{1,0:T(8,128)(2,1)}, bf16[512,512]{1,0:T(8,128)(2,1)}, bf16[2,2,512,256]{3,2,1,0:T(8,128)(2,1)}, f32[1,512]{1,0:T(1,128)}) custom-call(bf16[512,512]{1,0:T(8,128)(2,1)} %feats_h.1, bf16[512,512]{1,0:T(8,128)(2,1)} %w_self_h.1, bf16[512,512]{1,0:T(8,128)(2,1)} %w_neigh_h.1, f32[1,512]{1,0:T(1,128)} %bitcast.16, ...), custom_call_target="tpu_custom_call" | custom-call | tf_op jit(solution)/shard_map/pallas_call | solution.py:451
  88.5 2.8 %shard_map.147 = (bf16[512,512]{1,0:T(8,128)(2,1)}, bf16[512,512]{1,0:T(8,128)(2,1)}, f32[512,512]{1,0:T(8,128)}, f32[512,512]{1,0:T(8,128)}, f32[1,512]{1,0:T(1,128)}) custom-call(bf16[512,512]{1,0:T(8,128)(2,1)} %get-tuple-element.14.out_v, bf16[512,512]{1,0:T(8,128)(2,1)} %get-tuple-element.15.gfeat_v, ...), custom_call_target="tpu_custom_call" | custom-call | tf_op jit(solution)/shard_map/pallas_call | solution.py:497

commit v4 on v3

--- a/solution.py
+++ b/solution.py
@@ -339,13 +339,13 @@
     ]
     core_stage(0)
     core_stage(1)
+    x_stage(0)
     stores[0].start()
     member_back(0)
+    x_stage(1)
     member_back(1)
-    x_stage(0)
     member_back(2)
     member_back(3)
-    x_stage(1)
     own[...] = dot(low[...], w_self[...], 1, 1)
     y_stage(0)
     y_stage(1)

time: 91.4 us -> 91.2 us (level)
  no operation moved by 1% of the time
where the time goes in v4:
time: 91.2 us; the launch traced here: 91.1 us
  Pallas kernels  90.4 us (99%)
    pallas_call x1, Pallas kernels, shards(): pl.pallas_call(functools.partial(kernel, groups, members, nx, cap), out_s...  87.7 us
    pallas_call x1, Pallas kernels, shards(): pl.pallas_call(finish, out_shape=(S((nodes, width), BF), S((nodes, width)...  2.77 us

profile of v4, /device:TPU:1, one launch (start us, length us, event | category | flops | bytes accessed | tf_op | source)
XLA Modules:
  0.0 91.1 jit_solution(10414519044653308599)
XLA Ops:
  0.6 87.7 %shard_map.146 = (bf16[512,512]{1,0:T(8,128)(2,1)}, bf16[512,512]{1,0:T(8,128)(2,1)}, bf16[2,2,512,256]{3,2,1,0:T(8,128)(2,1)}, f32[1,512]{1,0:T(1,128)}) custom-call(bf16[512,512]{1,0:T(8,128)(2,1)} %feats_h.1, bf16[512,512]{1,0:T(8,128)(2,1)} %w_self_h.1, bf16[512,512]{1,0:T(8,128)(2,1)} %w_neigh_h.1, f32[1,512]{1,0:T(1,128)} %bitcast.16, ...), custom_call_target="tpu_custom_call" | custom-call | tf_op jit(solution)/shard_map/pallas_call | solution.py:451
  88.3 2.8 %shard_map.147 = (bf16[512,512]{1,0:T(8,128)(2,1)}, bf16[512,512]{1,0:T(8,128)(2,1)}, f32[512,512]{1,0:T(8,128)}, f32[512,512]{1,0:T(8,128)}, f32[1,512]{1,0:T(1,128)}) custom-call(bf16[512,512]{1,0:T(8,128)(2,1)} %get-tuple-element.14.out_v, bf16[512,512]{1,0:T(8,128)(2,1)} %get-tuple-element.15.gfeat_v, ...), custom_call_target="tpu_custom_call" | custom-call | tf_op jit(solution)/shard_map/pallas_call | solution.py:497
